TPU v7x, 1024 devices: a whole 8x8x8 slice. The times are simulated.
1024 devices in a mesh: slab: 128 (over y, z, core), face: 8 (over x).
Axes of the slice: x: 8, y: 8, z: 8, core: 2. Of those that a mesh axis runs over, the one named last changes fastest.
Arguments:
- a_blocks: bfloat16 [8192, 7, 128, 128], P(('slab', 'face')), may hold values from -0.5 to 0.5
- columns: int32 [8192, 7], P(('slab', 'face')), may hold values from 0 to 31
- counts: int32 [8192], P(('slab', 'face')), may hold values from 1 to 7, as said below
- p_blocks: bfloat16 [8192, 128, 128], P(('slab', 'face')), may hold values from -1 to 1
- aggregate: int32 [8192], P(('slab', 'face')), may hold values from 0 to 1
- readers: int32 [1024, 4, 6], P(('slab', 'face')), may hold values from 0 to 7
Outputs:
- coarse: float32 [2048, 5, 2, 128, 128], P(('slab', 'face'))
Inputs may be any that keep to these rules, and one draw needn't show every extreme that they name: Each device has some fine row with 7 live slots; devices differ in their typical counts.
All inputs are finite; a program needn't handle non-finite values.
Results may differ from a plain program's by a relative error of at most 0.01.
Values may be sent and summed in bfloat16 or wider, within the bound.
A program may use at most 32 MiB of HBM per device.

v0:
```python
import jax
import jax.numpy as jnp
from jax import lax
from jax.sharding import PartitionSpec as P

CBD = 2


def shifted(value, axis, steps):
    count = lax.axis_size(axis)
    initial, last = (max(0, -steps), min(count, count - steps))
    return lax.ppermute(value, axis, [(source, source + steps) for source in range(initial, last)])


def body(a_blocks, columns, counts, p_blocks, aggregate, readers):
    fine = p_blocks.shape[0]
    lists = readers.shape[2]
    kmax = a_blocks.shape[1]
    width = p_blocks.shape[1]
    groups = 5 * CBD
    pools = [p_blocks]
    pool_aggs = [aggregate]
    for by_step, entry in ((1, 1), (-1, 0)):
        got_p, got_agg, got_list = shifted(
            (p_blocks, aggregate, readers[0, entry]), "slab", by_step
        )
        pools.append(got_p[got_list])
        pool_aggs.append(got_agg[got_list])
    for by_step, entry in ((1, 3), (-1, 2)):
        got_p, got_agg, got_list = shifted(
            (p_blocks, aggregate, readers[0, entry]), "face", by_step
        )
        pools.append(got_p[got_list])
        pool_aggs.append(got_agg[got_list])
    pool = jnp.concatenate(pools, axis=0)
    pool_agg = jnp.concatenate(pool_aggs, axis=0)
    direction = jnp.where(columns < fine, 0, 1 + (columns - fine) // lists)
    group = direction * CBD + pool_agg[columns]
    live = jnp.arange(kmax)[None, :] < counts[:, None]
    onehot = ((group[..., None] == jnp.arange(groups)[None, None, :]) & live[..., None]).astype(
        jnp.float32
    )
    picked = pool[columns]
    agg_hot = (aggregate[:, None] == jnp.arange(CBD)[None, :]).astype(jnp.float32)
    step_rows = 4
    turns = fine // step_rows

    def regroup(array):
        return array.reshape((turns, step_rows) + array.shape[1:])

    def accumulate(total, pieces):
        a_part, picked_part, hot_part, p_part, agg_part = pieces
        prod = jnp.einsum(
            "ikrs,ikst->ikrt", a_part, picked_part, preferred_element_type=jnp.float32
        )
        q_blocks = jnp.einsum("ikg,ikrt->igrt", hot_part, prod).astype(jnp.bfloat16)
        z_blocks = jnp.einsum(
            "isr,igst->igrt", p_part, q_blocks, preferred_element_type=jnp.float32
        )
        return (total + jnp.einsum("ia,igrt->agrt", agg_part, z_blocks), None)

    start = jnp.zeros((CBD, groups, width, width), jnp.float32)
    total, unused = lax.scan(
        accumulate,
        start,
        (regroup(a_blocks), regroup(picked), regroup(onehot), regroup(p_blocks), regroup(agg_hot)),
    )
    return total.reshape(CBD, 5, CBD, width, width)


def solution(mesh):
    in_specs = (
        P(("slab", "face"), None, None, None),
        P(("slab", "face"), None),
        P(("slab", "face")),
        P(("slab", "face"), None, None),
        P(("slab", "face")),
        P(("slab", "face"), None, None),
    )
    out_specs = P(("slab", "face"), None, None, None, None)
    return jax.shard_map(body, mesh=mesh, in_specs=in_specs, out_specs=out_specs, check_vma=False)
```

profile of v0, /device:TPU:70, one launch (start us, length us, event | category | flops | bytes accessed | tf_op | source)
XLA Modules:
  0.0 101.3 jit_solution(3735510606277968143)
XLA Ops:
  0.0 2.0 %collective-permute-start.8 = (bf16[8,128,128]{2,1,0:T(8,128)(2,1)}, bf16[8,128,128]{2,1,0:T(8,128)(2,1)S(1)}, u32[]{:S(2)}, u32[]{:S(2)}) collective-permute-start(bf16[8,128,128]{2,1,0:T(8,128)(2,1)} %param.11), channel_id=1, source_target_pairs={{0,8},{8,16},{16,24},{24,32},{32,40},{40,48},{48,56},{56,64},{64,7... | collective-permute-start | bytes 786440 | tf_op jit(solution)/shard_map/ppermute | solution.py:12
  2.1 16.5 %collective-permute-start.9 = (bf16[8,128,128]{2,1,0:T(8,128)(2,1)}, bf16[8,128,128]{2,1,0:T(8,128)(2,1)S(1)}, u32[]{:S(2)}, u32[]{:S(2)}) collective-permute-start(bf16[8,128,128]{2,1,0:T(8,128)(2,1)} %param.11), channel_id=1, source_target_pairs={{8,0},{16,8},{24,16},{32,24},{40,32},{48,40},{56,48},{64,56},{72,6... | collective-permute-start | bytes 786440 | tf_op jit(solution)/shard_map/ppermute | solution.py:12
  18.6 4.6 %collective-permute-start.10 = (bf16[8,128,128]{2,1,0:T(8,128)(2,1)}, bf16[8,128,128]{2,1,0:T(8,128)(2,1)S(1)}, u32[]{:S(2)}, u32[]{:S(2)}) collective-permute-start(bf16[8,128,128]{2,1,0:T(8,128)(2,1)} %param.11), channel_id=1, source_target_pairs={{0,1},{1,2},{2,3},{3,4},{4,5},{5,6},{6,7},{8,9},{9,10},{10,11},{11... | collective-permute-start | bytes 786440 | tf_op jit(solution)/shard_map/ppermute | solution.py:12
  23.2 1.9 %collective-permute-start.11 = (bf16[8,128,128]{2,1,0:T(8,128)(2,1)}, bf16[8,128,128]{2,1,0:T(8,128)(2,1)S(1)}, u32[]{:S(2)}, u32[]{:S(2)}) collective-permute-start(bf16[8,128,128]{2,1,0:T(8,128)(2,1)} %param.11), channel_id=1, source_target_pairs={{1,0},{2,1},{3,2},{4,3},{5,4},{6,5},{7,6},{9,8},{10,9},{11,10},{12... | collective-permute-start | bytes 786440 | tf_op jit(solution)/shard_map/ppermute | solution.py:12
  25.1 0.8 slice_bitcast_fusion
  26.0 1.9 %collective-permute-start.1 = (s32[6]{0:T(128)S(1)}, s32[6]{0:T(128)S(1)}, u32[]{:S(2)}, u32[]{:S(2)}) collective-permute-start(s32[6]{0:T(128)S(1)} %get-tuple-element.83), channel_id=1, source_target_pairs={{0,8},{8,16},{16,24},{24,32},{32,40},{40,48},{48,56},{56,64},{64,7... | collective-permute-start | bytes 80 | tf_op jit(solution)/shard_map/ppermute | solution.py:12
  27.9 1.0 constant_dynamic-update-slice_fusion.4
  31.2 3.0 %collective-permute-done.1 = s32[6]{0:T(128)S(1)} collective-permute-done((s32[6]{0:T(128)S(1)}, s32[6]{0:T(128)S(1)}, u32[]{:S(2)}, u32[]{:S(2)}) %collective-permute-start.1) | collective-permute-done | bytes 56 | tf_op jit(solution)/shard_map/ppermute | solution.py:12
  34.2 4.0 %collective-permute-start.3 = (s32[6]{0:T(128)S(1)}, s32[6]{0:T(128)S(1)}, u32[]{:S(2)}, u32[]{:S(2)}) collective-permute-start(s32[6]{0:T(128)S(1)} %get-tuple-element.82), channel_id=1, source_target_pairs={{8,0},{16,8},{24,16},{32,24},{40,32},{48,40},{56,48},{64,56},{72,6... | collective-permute-start | bytes 80 | tf_op jit(solution)/shard_map/ppermute | solution.py:12
  38.2 1.2 %collective-permute-done.3 = s32[6]{0:T(128)S(1)} collective-permute-done((s32[6]{0:T(128)S(1)}, s32[6]{0:T(128)S(1)}, u32[]{:S(2)}, u32[]{:S(2)}) %collective-permute-start.3) | collective-permute-done | bytes 56 | tf_op jit(solution)/shard_map/ppermute | solution.py:12
  39.4 5.1 %collective-permute-start.5 = (s32[6]{0:T(128)S(1)}, s32[6]{0:T(128)S(1)}, u32[]{:S(2)}, u32[]{:S(2)}) collective-permute-start(s32[6]{0:T(128)S(1)} %get-tuple-element.84), channel_id=1, source_target_pairs={{0,1},{1,2},{2,3},{3,4},{4,5},{5,6},{6,7},{8,9},{9,10},{10,11},{11... | collective-permute-start | bytes 80 | tf_op jit(solution)/shard_map/ppermute | solution.py:12
  44.6 1.2 %collective-permute-done.5 = s32[6]{0:T(128)S(1)} collective-permute-done((s32[6]{0:T(128)S(1)}, s32[6]{0:T(128)S(1)}, u32[]{:S(2)}, u32[]{:S(2)}) %collective-permute-start.5) | collective-permute-done | bytes 56 | tf_op jit(solution)/shard_map/ppermute | solution.py:12
  45.8 1.9 %collective-permute-start.7 = (s32[6]{0:T(128)S(1)}, s32[6]{0:T(128)S(1)}, u32[]{:S(2)}, u32[]{:S(2)}) collective-permute-start(s32[6]{0:T(128)S(1)} %get-tuple-element.81), channel_id=1, source_target_pairs={{1,0},{2,1},{3,2},{4,3},{5,4},{6,5},{7,6},{9,8},{10,9},{11,10},{12... | collective-permute-start | bytes 80 | tf_op jit(solution)/shard_map/ppermute | solution.py:12
  47.7 4.9 %collective-permute-done.7 = s32[6]{0:T(128)S(1)} collective-permute-done((s32[6]{0:T(128)S(1)}, s32[6]{0:T(128)S(1)}, u32[]{:S(2)}, u32[]{:S(2)}) %collective-permute-start.7) | collective-permute-done | bytes 56 | tf_op jit(solution)/shard_map/ppermute | solution.py:12
  52.7 1.9 %collective-permute-start = (s32[8]{0:T(128)}, s32[8]{0:T(128)S(1)}, u32[]{:S(2)}, u32[]{:S(2)}) collective-permute-start(s32[8]{0:T(128)} %param.12), channel_id=1, source_target_pairs={{0,8},{8,16},{16,24},{24,32},{32,40},{40,48},{48,56},{56,64},{64,7... | collective-permute-start | bytes 104 | tf_op jit(solution)/shard_map/ppermute | solution.py:12
  54.6 6.4 %collective-permute-done = s32[8]{0:T(128)S(1)} collective-permute-done((s32[8]{0:T(128)}, s32[8]{0:T(128)S(1)}, u32[]{:S(2)}, u32[]{:S(2)}) %collective-permute-start) | collective-permute-done | bytes 64 | tf_op jit(solution)/shard_map/ppermute | solution.py:12
  61.0 1.9 %collective-permute-start.2 = (s32[8]{0:T(128)}, s32[8]{0:T(128)S(1)}, u32[]{:S(2)}, u32[]{:S(2)}) collective-permute-start(s32[8]{0:T(128)} %param.12), channel_id=1, source_target_pairs={{8,0},{16,8},{24,16},{32,24},{40,32},{48,40},{56,48},{64,56},{72,6... | collective-permute-start | bytes 104 | tf_op jit(solution)/shard_map/ppermute | solution.py:12
  64.3 3.9 %collective-permute-start.4 = (s32[8]{0:T(128)}, s32[8]{0:T(128)S(1)}, u32[]{:S(2)}, u32[]{:S(2)}) collective-permute-start(s32[8]{0:T(128)} %param.12), channel_id=1, source_target_pairs={{0,1},{1,2},{2,3},{3,4},{4,5},{5,6},{6,7},{8,9},{9,10},{10,11},{11... | collective-permute-start | bytes 104 | tf_op jit(solution)/shard_map/ppermute | solution.py:12
  68.9 1.0 collective-permute-done.4
  69.9 1.9 %collective-permute-start.6 = (s32[8]{0:T(128)S(1)}, s32[8]{0:T(128)S(1)}, u32[]{:S(2)}, u32[]{:S(2)}) collective-permute-start(s32[8]{0:T(128)S(1)} %copy-done.2), channel_id=1, source_target_pairs={{1,0},{2,1},{3,2},{4,3},{5,4},{6,5},{7,6},{9,8},{10,9},{11,10},{12... | collective-permute-start | bytes 104 | tf_op jit(solution)/shard_map/ppermute | solution.py:12
  72.4 4.1 %collective-permute-done.6 = s32[8]{0:T(128)S(1)} collective-permute-done((s32[8]{0:T(128)S(1)}, s32[8]{0:T(128)S(1)}, u32[]{:S(2)}, u32[]{:S(2)}) %collective-permute-start.6) | collective-permute-done | bytes 64 | tf_op jit(solution)/shard_map/ppermute | solution.py:12
  80.9 2.1 %gather_fusion.9 = bf16[56,128,128]{2,1,0:T(8,128)(2,1)} fusion(bf16[32,128,128]{2,1,0:T(8,128)(2,1)S(1)} %constant_dynamic-update-slice_fusion, s32[1024]{0:T(1024)S(1)} %pad_clamp_fusion), kind=kCustom, calls=%fused_computation.9 | custom fusion | bytes 3670240 | tf_op jit(solution)/shard_map/gather | solution.py:43
  83.0 15.8 %while.11 = (s32[]{:T(128)}, f32[2,10,128,128]{3,0,2,1:T(2,128)}, bf16[2,4,2]{1,2,0:T(2,128)(2,1)S(1)}, bf16[2,4,7,10]{3,1,2,0:T(4,128)(2,1)S(1)}, bf16[2,4,7,12...) while((s32[]{:T(128)}, f32[2,10,128,128]{3,0,2,1:T(2,128)}, ...), condition=%wide.region_1.2_spmd.clone, body=%wide.region_0.1_spmd.clone.sunk | while | flops 297664512 | bytes 15076611 | solution.py:63
  83.0 1.9 %fusion.45 = bf16[4,7,128,128]{3,2,1,0:T(8,128)(2,1)S(1)} fusion(bf16[2,4,7,128,128]{4,3,2,1,0:T(8,128)(2,1)} %get-tuple-element.151, s32[]{:T(128)} %get-tuple-element.137, bf16[2,4,7,128,128]{4,3,2,1,0:T(8,128)(2,1)} %get-tuple-element.150), kind=kOutput, calls=%fused_computation.17.clone.1 | convolution fusion | flops 117440512 | bytes 2753536 | tf_op jit(solution)/shard_map/while/body/eval_jaxpr/ikrs,ikst->ikrt/dot_general | solution.py:53
  84.9 0.9 fusion.46
  86.4 1.7 %copy.30 = bf16[4,10,128,128]{2,0,3,1:T(4,128)(2,1)S(1)} copy(bf16[4,10,128,128]{3,2,1,0:T(8,128)(2,1)S(1)} %fusion.47) | data formatting | bytes 2621440 | tf_op jit(solution)/shard_map/while/body/eval_jaxpr/isr,igst->igrt/dot_general | solution.py:57
  88.2 2.0 %fusion.48 = f32[2,10,128,128]{3,0,2,1:T(2,128)} fusion(bf16[4,10,128,128]{2,0,3,1:T(4,128)(2,1)S(1)} %copy.30, f32[2,10,128,128]{3,0,2,1:T(2,128)} %get-tuple-element.138, pred[]{:T(512)S(6)} %compare.3, bf16[2,4,2]{1,2,0:T(2,128)(2,1)S(1)} %get-tuple-element.148, s32[]{:T(128)} %get-tuple-element.137), kind=kOutput, calls=%fused_computation.15.clone.1 | convolution fusion | flops 3276800 | bytes 3932677 | tf_op jit(solution)/shard_map/while/body/eval_jaxpr/ia,igrt->agrt/dot_general | solution.py:60
  90.2 1.8 %fusion.45 = bf16[4,7,128,128]{3,2,1,0:T(8,128)(2,1)S(1)} fusion(bf16[2,4,7,128,128]{4,3,2,1,0:T(8,128)(2,1)} %get-tuple-element.151, s32[]{:T(128)} %get-tuple-element.137, bf16[2,4,7,128,128]{4,3,2,1,0:T(8,128)(2,1)} %get-tuple-element.150), kind=kOutput, calls=%fused_computation.17.clone.1 | convolution fusion | flops 117440512 | bytes 2753536 | tf_op jit(solution)/shard_map/while/body/eval_jaxpr/ikrs,ikst->ikrt/dot_general | solution.py:53
  92.1 0.9 fusion.46
  93.6 1.7 %copy.30 = bf16[4,10,128,128]{2,0,3,1:T(4,128)(2,1)S(1)} copy(bf16[4,10,128,128]{3,2,1,0:T(8,128)(2,1)S(1)} %fusion.47) | data formatting | bytes 2621440 | tf_op jit(solution)/shard_map/while/body/eval_jaxpr/isr,igst->igrt/dot_general | solution.py:57
  95.4 3.4 %fusion.48 = f32[2,10,128,128]{3,0,2,1:T(2,128)} fusion(bf16[4,10,128,128]{2,0,3,1:T(4,128)(2,1)S(1)} %copy.30, f32[2,10,128,128]{3,0,2,1:T(2,128)} %get-tuple-element.138, pred[]{:T(512)S(6)} %compare.3, bf16[2,4,2]{1,2,0:T(2,128)(2,1)S(1)} %get-tuple-element.148, s32[]{:T(128)} %get-tuple-element.137), kind=kOutput, calls=%fused_computation.15.clone.1 | convolution fusion | flops 3276800 | bytes 3932677 | tf_op jit(solution)/shard_map/while/body/eval_jaxpr/ia,igrt->agrt/dot_general | solution.py:60
  98.7 2.5 %copy.10 = f32[2,10,128,128]{3,2,1,0:T(8,128)} copy(f32[2,10,128,128]{3,0,2,1:T(2,128)} %get-tuple-element.42) | data formatting | bytes 2621440 | tf_op jit(solution)/shard_map/while | solution.py:63
  (49 shorter events, 10.6 us)
Async XLA Ops:
  0.0 69.9 %copy-start.2 = (s32[8]{0:T(128)S(1)}, s32[8]{0:T(128)}, u32[]{:S(2)}) copy-start(s32[8]{0:T(128)} %param.12) | copy-start | bytes 100
  0.0 78.3 %collective-permute-start.8 = (bf16[8,128,128]{2,1,0:T(8,128)(2,1)}, bf16[8,128,128]{2,1,0:T(8,128)(2,1)S(1)}, u32[]{:S(2)}, u32[]{:S(2)}) collective-permute-start(bf16[8,128,128]{2,1,0:T(8,128)(2,1)} %param.11), channel_id=1, source_target_pairs={{0,8},{8,16},{16,24},{24,32},{32,40},{40,48},{48,56},{56,64},{64,7... | collective-permute-start | bytes 786440 | tf_op jit(solution)/shard_map/ppermute | solution.py:12
  2.1 76.9 %collective-permute-start.9 = (bf16[8,128,128]{2,1,0:T(8,128)(2,1)}, bf16[8,128,128]{2,1,0:T(8,128)(2,1)S(1)}, u32[]{:S(2)}, u32[]{:S(2)}) collective-permute-start(bf16[8,128,128]{2,1,0:T(8,128)(2,1)} %param.11), channel_id=1, source_target_pairs={{8,0},{16,8},{24,16},{32,24},{40,32},{48,40},{56,48},{64,56},{72,6... | collective-permute-start | bytes 786440 | tf_op jit(solution)/shard_map/ppermute | solution.py:12
  18.6 61.0 %collective-permute-start.10 = (bf16[8,128,128]{2,1,0:T(8,128)(2,1)}, bf16[8,128,128]{2,1,0:T(8,128)(2,1)S(1)}, u32[]{:S(2)}, u32[]{:S(2)}) collective-permute-start(bf16[8,128,128]{2,1,0:T(8,128)(2,1)} %param.11), channel_id=1, source_target_pairs={{0,1},{1,2},{2,3},{3,4},{4,5},{5,6},{6,7},{8,9},{9,10},{10,11},{11... | collective-permute-start | bytes 786440 | tf_op jit(solution)/shard_map/ppermute | solution.py:12
  23.2 57.0 %collective-permute-start.11 = (bf16[8,128,128]{2,1,0:T(8,128)(2,1)}, bf16[8,128,128]{2,1,0:T(8,128)(2,1)S(1)}, u32[]{:S(2)}, u32[]{:S(2)}) collective-permute-start(bf16[8,128,128]{2,1,0:T(8,128)(2,1)} %param.11), channel_id=1, source_target_pairs={{1,0},{2,1},{3,2},{4,3},{5,4},{6,5},{7,6},{9,8},{10,9},{11,10},{12... | collective-permute-start | bytes 786440 | tf_op jit(solution)/shard_map/ppermute | solution.py:12
  26.0 8.2 %collective-permute-start.1 = (s32[6]{0:T(128)S(1)}, s32[6]{0:T(128)S(1)}, u32[]{:S(2)}, u32[]{:S(2)}) collective-permute-start(s32[6]{0:T(128)S(1)} %get-tuple-element.83), channel_id=1, source_target_pairs={{0,8},{8,16},{16,24},{24,32},{32,40},{40,48},{48,56},{56,64},{64,7... | collective-permute-start | bytes 80 | tf_op jit(solution)/shard_map/ppermute | solution.py:12
  34.2 5.2 %collective-permute-start.3 = (s32[6]{0:T(128)S(1)}, s32[6]{0:T(128)S(1)}, u32[]{:S(2)}, u32[]{:S(2)}) collective-permute-start(s32[6]{0:T(128)S(1)} %get-tuple-element.82), channel_id=1, source_target_pairs={{8,0},{16,8},{24,16},{32,24},{40,32},{48,40},{56,48},{64,56},{72,6... | collective-permute-start | bytes 80 | tf_op jit(solution)/shard_map/ppermute | solution.py:12
  39.4 6.4 %collective-permute-start.5 = (s32[6]{0:T(128)S(1)}, s32[6]{0:T(128)S(1)}, u32[]{:S(2)}, u32[]{:S(2)}) collective-permute-start(s32[6]{0:T(128)S(1)} %get-tuple-element.84), channel_id=1, source_target_pairs={{0,1},{1,2},{2,3},{3,4},{4,5},{5,6},{6,7},{8,9},{9,10},{10,11},{11... | collective-permute-start | bytes 80 | tf_op jit(solution)/shard_map/ppermute | solution.py:12
  45.8 6.9 %collective-permute-start.7 = (s32[6]{0:T(128)S(1)}, s32[6]{0:T(128)S(1)}, u32[]{:S(2)}, u32[]{:S(2)}) collective-permute-start(s32[6]{0:T(128)S(1)} %get-tuple-element.81), channel_id=1, source_target_pairs={{1,0},{2,1},{3,2},{4,3},{5,4},{6,5},{7,6},{9,8},{10,9},{11,10},{12... | collective-permute-start | bytes 80 | tf_op jit(solution)/shard_map/ppermute | solution.py:12
  52.7 8.3 %collective-permute-start = (s32[8]{0:T(128)}, s32[8]{0:T(128)S(1)}, u32[]{:S(2)}, u32[]{:S(2)}) collective-permute-start(s32[8]{0:T(128)} %param.12), channel_id=1, source_target_pairs={{0,8},{8,16},{16,24},{24,32},{32,40},{40,48},{48,56},{56,64},{64,7... | collective-permute-start | bytes 104 | tf_op jit(solution)/shard_map/ppermute | solution.py:12
  61.0 3.3 %collective-permute-start.2 = (s32[8]{0:T(128)}, s32[8]{0:T(128)S(1)}, u32[]{:S(2)}, u32[]{:S(2)}) collective-permute-start(s32[8]{0:T(128)} %param.12), channel_id=1, source_target_pairs={{8,0},{16,8},{24,16},{32,24},{40,32},{48,40},{56,48},{64,56},{72,6... | collective-permute-start | bytes 104 | tf_op jit(solution)/shard_map/ppermute | solution.py:12
  64.3 5.6 %collective-permute-start.4 = (s32[8]{0:T(128)}, s32[8]{0:T(128)S(1)}, u32[]{:S(2)}, u32[]{:S(2)}) collective-permute-start(s32[8]{0:T(128)} %param.12), channel_id=1, source_target_pairs={{0,1},{1,2},{2,3},{3,4},{4,5},{5,6},{6,7},{8,9},{9,10},{10,11},{11... | collective-permute-start | bytes 104 | tf_op jit(solution)/shard_map/ppermute | solution.py:12
  69.9 6.6 %collective-permute-start.6 = (s32[8]{0:T(128)S(1)}, s32[8]{0:T(128)S(1)}, u32[]{:S(2)}, u32[]{:S(2)}) collective-permute-start(s32[8]{0:T(128)S(1)} %copy-done.2), channel_id=1, source_target_pairs={{1,0},{2,1},{3,2},{4,3},{5,4},{6,5},{7,6},{9,8},{10,9},{11,10},{12... | collective-permute-start | bytes 104 | tf_op jit(solution)/shard_map/ppermute | solution.py:12
  77.2 0.9 copy-start.1
  80.9 2.1 %copy-start = (bf16[8,128,128]{2,1,0:T(8,128)(2,1)S(1)}, bf16[8,128,128]{2,1,0:T(8,128)(2,1)}, u32[]{:S(2)}) copy-start(bf16[8,128,128]{2,1,0:T(8,128)(2,1)} %param.11) | copy-start | bytes 786436
where the time goes:
time: 102 us; the launch traced here: 101 us
  starting transfers between devices  47.7 us (47%)
  waiting for transfers between devices  22.6 us (22%)
  local copies, waits for them, and re-layouts  17.5 us (17%)
  matrix products  12.2 us (12%)
    ppermute x12, starting transfers between devices, shifted(): lax.ppermute(value, axis, [(source, source + steps) for source in range(i...  47.7 us
    ppermute x12, waiting for transfers between devices, shifted(): lax.ppermute(value, axis, [(source, source + steps) for source in range(i...  22.6 us
    dot_general x2, matrix products, accumulate(): return (total + jnp.einsum('ia,igrt->agrt', agg_part, z_blocks), None)  5.39 us
    dot_general x2, matrix products, accumulate(): jnp.einsum('ikrs,ikst->ikrt', a_part, picked_part, preferred_element_type...  3.72 us
    dot_general x2, local copies, waits for them, and re-layouts, accumulate(): jnp.einsum('isr,igst->igrt', p_part, q_blocks, preferred_element_type=jnp...  3.45 us
    gather x4, local copies, waits for them, and re-layouts, body(): pool_aggs.append(got_agg[got_list])  2.57 us
    while x1, local copies, waits for them, and re-layouts, body(): lax.scan(accumulate, start, (regroup(a_blocks), regroup(picked), regroup(...  2.53 us
    gather x4, local copies, waits for them, and re-layouts, body(): pools.append(got_p[got_list])  2.34 us
  transfers between devices with their start and end apart: 12, of which 8 were waited for; matrix products, arithmetic and copies ran while one was open for 10% of the time, Pallas kernels for 0%

commit v1 on v0

v1 whole, which is shorter than its diff:
```python
import functools

import jax
import jax.numpy as jnp
from jax import lax
from jax.experimental import pallas as pl
from jax.experimental.pallas import tpu as pltpu
from jax.sharding import PartitionSpec as P

MESH = pl.DeviceIdType.MESH
CBD = 2
FB = 8
KMAX = 7
RL = 6
B = 128
COLS = FB + 4 * RL
SLOTS = FB * KMAX


def neighbours():
    slab, face = lax.axis_index("slab"), lax.axis_index("face")
    n_slab, n_face = lax.axis_size("slab"), lax.axis_size("face")
    return (
        (slab >= 1, (slab - 1, face)),
        (slab + 1 < n_slab, (slab + 1, face)),
        (face >= 1, (slab, face - 1)),
        (face + 1 < n_face, (slab, face + 1)),
    )


def kernel(
    columns, counts, aggregate, readers, a_hbm, p_hbm, out_hbm,
    p, a, send, recv, send_mask, recv_mask, keys, links, table, sums, c, x, out,
    p_sem, a_sem, table_sem, out_sem, send_sem, recv_sem, send_mask_sem, recv_mask_sem,
):
    around = neighbours()
    barrier = pltpu.get_barrier_semaphore()
    for there, device in around:
        @pl.when(there)
        def _():
            pl.semaphore_signal(barrier, inc=1, device_id=device, device_id_type=MESH)

    load_p = pltpu.make_async_copy(p_hbm, p, p_sem)
    load_p.start()
    load_a = [pltpu.make_async_copy(a_hbm.at[i], a.at[i], a_sem.at[i]) for i in range(FB)]
    for copy in load_a:
        copy.start()

    sublane = lax.broadcasted_iota(jnp.int32, (8, B), 0)
    blocks, masks = [], []
    for e in range(4):
        device = around[e][1]
        blocks.append(pltpu.make_async_remote_copy(
            src_ref=send.at[e], dst_ref=recv.at[e ^ 1], send_sem=send_sem.at[e],
            recv_sem=recv_sem.at[e ^ 1], device_id=device, device_id_type=MESH))
        masks.append(pltpu.make_async_remote_copy(
            src_ref=send_mask.at[e], dst_ref=recv_mask.at[e ^ 1], send_sem=send_mask_sem.at[e],
            recv_sem=recv_mask_sem.at[e ^ 1], device_id=device, device_id_type=MESH))
    load_p.wait()
    for n, e in enumerate((2, 3, 0, 1)):
        mask = jnp.zeros((8, B), jnp.int32)
        for r in range(RL):
            block = readers[0, e, r]
            send[e, r] = p[block]
            mask = jnp.where(sublane == r, aggregate[block], mask)
        send_mask[e] = mask.astype(jnp.float32)
        if n == 0:
            expected = sum(there.astype(jnp.int32) for there, unused in around)
            pl.semaphore_wait(barrier, expected)

        @pl.when(around[e][0])
        def _():
            masks[e].start()
            blocks[e].start()

    for i in range(FB):
        for k in range(KMAX):
            key = jnp.where(k < counts[i], aggregate[i] * COLS + columns[i, k], -1)
            m = i * KMAX + k
            keys[m:m + 1, :] = jnp.full((1, B), key, jnp.int32)
    keys[SLOTS:, :] = jnp.full((64 - SLOTS, B), -2, jnp.int32)
    by_row = keys[...]
    row = lax.broadcasted_iota(jnp.int32, (64, B), 0)
    lane = lax.broadcasted_iota(jnp.int32, (64, B), 1)
    by_lane = jnp.sum(jnp.where(row == lane, by_row, 0), axis=0, keepdims=True)
    before = jnp.where((by_row == by_lane) & (row < lane), row + 1, 0)
    links[0:1, :] = jnp.max(before, axis=0, keepdims=True)
    links[1:2, :] = jnp.max(jnp.where(by_row == lane, row + 1, 0), axis=0, keepdims=True)
    links[2:, :] = jnp.zeros((6, B), jnp.int32)
    load_table = pltpu.make_async_copy(links, table, table_sem)
    load_table.start()
    sums[0] = jnp.zeros((B, B), jnp.float32)
    load_table.wait()

    def accumulate(i, carry):
        pltpu.make_async_copy(a_hbm.at[i], a.at[i], a_sem.at[i]).wait()
        wide = jnp.concatenate([a[i, k] for k in range(KMAX)], axis=1)
        product = jnp.dot(p[i].T, wide, preferred_element_type=jnp.float32)
        for k in range(KMAX):
            m = i * KMAX + k
            sums[m + 1] = product[:, k * B:(k + 1) * B] + sums[table[0, m]]
        return carry

    lax.fori_loop(0, FB, accumulate, 0)

    def collect(j, carry):
        c[j, 0:B, :] = sums[table[1, j]].astype(jnp.bfloat16)
        c[j, B:2 * B, :] = sums[table[1, COLS + j]].astype(jnp.bfloat16)
        return carry

    lax.fori_loop(0, COLS, collect, 0)

    stores = []

    def finish(d, first, number):
        left = jnp.concatenate([c[first + j] for j in range(number)], axis=1)
        total = jnp.dot(left, x[0:number * B, :], preferred_element_type=jnp.float32)
        for owner in range(CBD):
            for b in range(CBD):
                out[owner, d, b] = total[owner * B:(owner + 1) * B, b * B:(b + 1) * B]
            store = pltpu.make_async_copy(
                out.at[owner, d], out_hbm.at[owner, d], out_sem.at[owner, d])
            store.start()
            stores.append(store)

    def split(j, block, mask):
        high = block * mask
        x[j * B:(j + 1) * B, B:] = high
        x[j * B:(j + 1) * B, :B] = block - high

    for j in range(FB):
        mask = jnp.full((B, B), aggregate[j], jnp.int32).astype(jnp.float32).astype(jnp.bfloat16)
        split(j, p[j], mask)
    finish(0, 0, FB)

    for q in range(4):
        there = around[q][0]

        @pl.when(there)
        def _():
            blocks[q ^ 1].wait_recv()
            masks[q ^ 1].wait_recv()
            for r in range(RL):
                mask = jnp.broadcast_to(recv_mask[q, r:r + 1, :], (B, B)).astype(jnp.bfloat16)
                split(r, recv[q, r], mask)

        @pl.when(jnp.logical_not(there))
        def _():
            x[0:RL * B, :] = jnp.zeros((RL * B, CBD * B), jnp.bfloat16)

        finish(q + 1, FB + q * RL, RL)

    for store in stores:
        store.wait()
    for e in range(4):
        @pl.when(around[e][0])
        def _():
            masks[e].wait_send()
            blocks[e].wait_send()


def body(a_blocks, columns, counts, p_blocks, aggregate, readers):
    smem = pl.BlockSpec(memory_space=pltpu.SMEM)
    anywhere = pl.BlockSpec(memory_space=pl.ANY)
    bf16, f32, i32 = jnp.bfloat16, jnp.float32, jnp.int32
    return pl.pallas_call(
        kernel,
        out_shape=jax.ShapeDtypeStruct((CBD, 5, CBD, B, B), f32),
        in_specs=[smem] * 4 + [anywhere] * 2,
        out_specs=anywhere,
        scratch_shapes=[
            pltpu.VMEM((FB, B, B), bf16),
            pltpu.VMEM((FB, KMAX, B, B), bf16),
            pltpu.VMEM((4, RL, B, B), bf16),
            pltpu.VMEM((4, RL, B, B), bf16),
            pltpu.VMEM((4, 8, B), f32),
            pltpu.VMEM((4, 8, B), f32),
            pltpu.VMEM((64, B), i32),
            pltpu.VMEM((8, B), i32),
            pltpu.SMEM((8, B), i32),
            pltpu.VMEM((SLOTS + 1, B, B), f32),
            pltpu.VMEM((COLS, CBD * B, B), bf16),
            pltpu.VMEM((FB * B, CBD * B), bf16),
            pltpu.VMEM((CBD, 5, CBD, B, B), f32),
            pltpu.SemaphoreType.DMA,
            pltpu.SemaphoreType.DMA((FB,)),
            pltpu.SemaphoreType.DMA,
            pltpu.SemaphoreType.DMA((CBD, 5)),
            pltpu.SemaphoreType.DMA((4,)),
            pltpu.SemaphoreType.DMA((4,)),
            pltpu.SemaphoreType.DMA((4,)),
            pltpu.SemaphoreType.DMA((4,)),
        ],
        compiler_params=pltpu.CompilerParams(
            collective_id=0, has_side_effects=True, vmem_limit_bytes=40 * 1024 * 1024
        ),
        cost_estimate=pl.CostEstimate(
            flops=700_000_000, bytes_accessed=3_500_000, transcendentals=0
        ),
        name="coarse_blocks",
    )(columns, counts, aggregate, readers, a_blocks, p_blocks)


def solution(mesh):
    in_specs = (
        P(("slab", "face"), None, None, None),
        P(("slab", "face"), None),
        P(("slab", "face")),
        P(("slab", "face"), None, None),
        P(("slab", "face")),
        P(("slab", "face"), None, None),
    )
    out_specs = P(("slab", "face"), None, None, None, None)
    return jax.shard_map(body, mesh=mesh, in_specs=in_specs, out_specs=out_specs, check_vma=False)
```

time: 102 us -> 32.6 us (0.32)
  the two profiles are of different devices: /device:TPU:70 before, /device:TPU:120 now
where the time goes in v1:
time: 32.6 us; the launch traced here: 32.4 us
  Pallas kernels  26.2 us (80%)
  local copies, waits for them, and re-layouts  6.18 us (19%)
    pallas_call x1, Pallas kernels, body(): pl.pallas_call(kernel, out_shape=jax.ShapeDtypeStruct((CBD, 5, CBD, B, B)...  26.2 us
    unnamed x13, local copies, waits for them, and re-layouts  6.18 us

profile of v1, /device:TPU:120, one launch (start us, length us, event | category | flops | bytes accessed | tf_op | source)
XLA Modules:
  0.0 32.4 jit_solution(17987277486657026572)
XLA Ops:
  0.0 0.0 copy-start
  0.0 1.5 %copy-done = bf16[8,7,128,128]{3,2,1,0:T(8,128)(2,1)S(1)} copy-done((bf16[8,7,128,128]{3,2,1,0:T(8,128)(2,1)S(1)}, bf16[8,7,128,128]{3,2,1,0:T(8,128)(2,1)}, u32[]{:S(2)}) %copy-start) | copy-done | bytes 1835032
  1.5 0.0 copy-start.1
  1.5 0.9 %copy-done.1 = bf16[8,128,128]{2,1,0:T(8,128)(2,1)S(1)} copy-done((bf16[8,128,128]{2,1,0:T(8,128)(2,1)S(1)}, bf16[8,128,128]{2,1,0:T(8,128)(2,1)}, u32[]{:S(2)}) %copy-start.1) | copy-done | bytes 262168
  2.5 0.0 copy-start.2
  2.5 0.7 %copy-done.2 = s32[8,7]{1,0:T(8,128)S(1)} copy-done((s32[8,7]{1,0:T(8,128)S(1)}, s32[8,7]{1,0:T(8,128)}, u32[]{:S(2)}) %copy-start.2) | copy-done | bytes 248
  3.1 0.0 copy-start.3
  3.1 0.7 %copy-done.3 = s32[1,4,6]{2,1,0:T(4,128)S(1)} copy-done((s32[1,4,6]{2,1,0:T(4,128)S(1)}, s32[1,4,6]{2,1,0:T(4,128)}, u32[]{:S(2)}) %copy-start.3) | copy-done | bytes 120
  3.8 0.0 copy-start.4
  3.8 0.7 %copy-done.4 = s32[8]{0:T(128)S(1)} copy-done((s32[8]{0:T(128)S(1)}, s32[8]{0:T(128)}, u32[]{:S(2)}) %copy-start.4) | copy-done | bytes 56
  4.5 0.0 copy-start.5
  4.5 0.7 %copy-done.5 = s32[8]{0:T(128)S(1)} copy-done((s32[8]{0:T(128)S(1)}, s32[8]{0:T(128)}, u32[]{:S(2)}) %copy-start.5) | copy-done | bytes 56
  5.1 26.2 %coarse_blocks.1 = f32[2,5,2,128,128]{4,3,2,1,0:T(8,128)S(1)} custom-call(s32[8,7]{1,0:T(8,128)S(1)} %copy-done.2, s32[8]{0:T(128)S(1)} %copy-done.4, s32[8]{0:T(128)S(1)} %copy-done.5, s32[1,4,6]{2,1,0:T(4,128)S(1)} %copy-done.3, bf16[8,7,128,128]{3,2,1,0:T(8,128)(2,1)S(1)} %copy-done, bf16[8,128,128]{2,1,0:T(8,128)(2,1)S(1)} %copy-done.1), custom_call_target="tpu_custom_call" | custom-call | flops 700000000 | bytes 3500000 | tf_op jit(solution)/shard_map/coarse_blocks/pallas_call | solution.py:166
  31.3 1.1 %copy.8 = f32[2,5,2,128,128]{4,3,2,1,0:T(8,128)} copy(f32[2,5,2,128,128]{4,3,2,1,0:T(8,128)S(1)} %coarse_blocks.1) | data formatting | bytes 2621440
Async XLA Ops:
  0.0 1.5 %copy-start = (bf16[8,7,128,128]{3,2,1,0:T(8,128)(2,1)S(1)}, bf16[8,7,128,128]{3,2,1,0:T(8,128)(2,1)}, u32[]{:S(2)}) copy-start(bf16[8,7,128,128]{3,2,1,0:T(8,128)(2,1)} %a_hbm.1) | copy-start | bytes 5505028
  1.5 0.9 %copy-start.1 = (bf16[8,128,128]{2,1,0:T(8,128)(2,1)S(1)}, bf16[8,128,128]{2,1,0:T(8,128)(2,1)}, u32[]{:S(2)}) copy-start(bf16[8,128,128]{2,1,0:T(8,128)(2,1)} %p_hbm.1) | copy-start | bytes 786436
  2.5 0.7 %copy-start.2 = (s32[8,7]{1,0:T(8,128)S(1)}, s32[8,7]{1,0:T(8,128)}, u32[]{:S(2)}) copy-start(s32[8,7]{1,0:T(8,128)} %columns.1) | copy-start | bytes 676
  3.1 0.7 %copy-start.3 = (s32[1,4,6]{2,1,0:T(4,128)S(1)}, s32[1,4,6]{2,1,0:T(4,128)}, u32[]{:S(2)}) copy-start(s32[1,4,6]{2,1,0:T(4,128)} %readers.1) | copy-start | bytes 292
  3.8 0.7 %copy-start.4 = (s32[8]{0:T(128)S(1)}, s32[8]{0:T(128)}, u32[]{:S(2)}) copy-start(s32[8]{0:T(128)} %counts.1) | copy-start | bytes 100
  4.5 0.7 %copy-start.5 = (s32[8]{0:T(128)S(1)}, s32[8]{0:T(128)}, u32[]{:S(2)}) copy-start(s32[8]{0:T(128)} %aggregate.1) | copy-start | bytes 100

commit v2 on v1

--- a/solution.py
+++ b/solution.py
@@ -15,36 +15,51 @@
 B = 128
 COLS = FB + 4 * RL
 SLOTS = FB * KMAX
+LINE = 8
 
 
 def neighbours():
     slab, face = lax.axis_index("slab"), lax.axis_index("face")
     n_slab, n_face = lax.axis_size("slab"), lax.axis_size("face")
+    odd = slab % 2 == 1
+    along = (slab // 2) % LINE
+    half = n_face // 2
+    corner = (slab == 0) & (face == 0)
+    beside = (slab == 0) & (face == 1)
+    above = (slab == 1) & (face == 0)
+    never = slab < 0
     return (
-        (slab >= 1, (slab - 1, face)),
-        (slab + 1 < n_slab, (slab + 1, face)),
-        (face >= 1, (slab, face - 1)),
-        (face + 1 < n_face, (slab, face + 1)),
+        (slab >= 1, (slab - 1, face), odd | (along == 0),
+         (jnp.logical_not(odd) & (along == 0)) | above),
+        (slab + 1 < n_slab, (slab + 1, face), odd & (along != LINE - 1), never),
+        (face >= 1, (slab, face - 1), (face > half) | beside, beside),
+        (face + 1 < n_face, (slab, face + 1), (face < half) & jnp.logical_not(corner), never),
     )
 
 
 def kernel(
-    columns, counts, aggregate, readers, a_hbm, p_hbm, out_hbm,
-    p, a, send, recv, send_mask, recv_mask, keys, links, table, sums, c, x, out,
-    p_sem, a_sem, table_sem, out_sem, send_sem, recv_sem, send_mask_sem, recv_mask_sem,
+    columns_hbm, counts_hbm, aggregate_hbm, readers_hbm, a_hbm, p_hbm, out,
+    columns, counts, aggregate, readers, p, a, send, recv, send_mask, recv_mask, keys, links, table, sums, c, x,
+    int_sem, p_sem, a_sem, table_sem, send_sem, recv_sem, send_mask_sem, recv_mask_sem, ready,
 ):
     around = neighbours()
+    load_lists = [
+        pltpu.make_async_copy(source, target, int_sem.at[n])
+        for n, (source, target) in enumerate((
+            (readers_hbm, readers), (aggregate_hbm, aggregate),
+            (counts_hbm, counts), (columns_hbm, columns)))
+    ]
+    load_p = pltpu.make_async_copy(p_hbm, p, p_sem)
+    load_a = [pltpu.make_async_copy(a_hbm.at[i], a.at[i], a_sem.at[i]) for i in range(FB)]
+    load_lists[0].start()
+    load_p.start()
+    for copy in load_lists[1:]:
+        copy.start()
     barrier = pltpu.get_barrier_semaphore()
-    for there, device in around:
-        @pl.when(there)
+    for there, device, later, unused in around:
+        @pl.when(there & later)
         def _():
             pl.semaphore_signal(barrier, inc=1, device_id=device, device_id_type=MESH)
-
-    load_p = pltpu.make_async_copy(p_hbm, p, p_sem)
-    load_p.start()
-    load_a = [pltpu.make_async_copy(a_hbm.at[i], a.at[i], a_sem.at[i]) for i in range(FB)]
-    for copy in load_a:
-        copy.start()
 
     sublane = lax.broadcasted_iota(jnp.int32, (8, B), 0)
     blocks, masks = [], []
@@ -56,22 +71,57 @@
         masks.append(pltpu.make_async_remote_copy(
             src_ref=send_mask.at[e], dst_ref=recv_mask.at[e ^ 1], send_sem=send_mask_sem.at[e],
             recv_sem=recv_mask_sem.at[e ^ 1], device_id=device, device_id_type=MESH))
-    load_p.wait()
-    for n, e in enumerate((2, 3, 0, 1)):
+
+    def pack(e):
         mask = jnp.zeros((8, B), jnp.int32)
         for r in range(RL):
             block = readers[0, e, r]
             send[e, r] = p[block]
             mask = jnp.where(sublane == r, aggregate[block], mask)
         send_mask[e] = mask.astype(jnp.float32)
-        if n == 0:
-            expected = sum(there.astype(jnp.int32) for there, unused in around)
-            pl.semaphore_wait(barrier, expected)
-
-        @pl.when(around[e][0])
+
+    def start(e, condition):
+        @pl.when(around[e][0] & condition)
         def _():
             masks[e].start()
             blocks[e].start()
+
+    def answer(e, condition):
+        there, unused, later, much = around[e]
+
+        @pl.when(there & later & condition)
+        def _():
+            pl.semaphore_wait(ready.at[e], 1)
+            masks[e].start()
+            blocks[e].start()
+
+    for copy in load_lists[:2]:
+        copy.wait()
+    load_p.wait()
+    pack(1)
+    before = [there & jnp.logical_not(later) for there, unused, later, much in around]
+    expected = sum(first.astype(jnp.int32) for first in before)
+
+    @pl.when(expected > 0)
+    def _():
+        pl.semaphore_wait(barrier, expected)
+
+    start(1, before[1])
+    for e in range(4):
+        @pl.when(before[e])
+        def _():
+            pl.semaphore_signal(
+                ready.at[e ^ 1], inc=1, device_id=around[e][1], device_id_type=MESH)
+    pack(0)
+    start(0, before[0])
+    pack(2)
+    start(2, before[2])
+    pack(3)
+    start(3, before[3])
+    for copy in load_a:
+        copy.start()
+    for copy in load_lists[2:]:
+        copy.wait()
 
     for i in range(FB):
         for k in range(KMAX):
@@ -90,6 +140,11 @@
     load_table = pltpu.make_async_copy(links, table, table_sem)
     load_table.start()
     sums[0] = jnp.zeros((B, B), jnp.float32)
+
+    soon = [jnp.logical_not(much) for unused, device, later, much in around]
+    answer(0, soon[0])
+    answer(3, soon[3])
+    answer(2, soon[2])
     load_table.wait()
 
     def accumulate(i, carry):
@@ -102,6 +157,7 @@
         return carry
 
     lax.fori_loop(0, FB, accumulate, 0)
+    answer(1, soon[1])
 
     def collect(j, carry):
         c[j, 0:B, :] = sums[table[1, j]].astype(jnp.bfloat16)
@@ -109,8 +165,6 @@
         return carry
 
     lax.fori_loop(0, COLS, collect, 0)
-
-    stores = []
 
     def finish(d, first, number):
         left = jnp.concatenate([c[first + j] for j in range(number)], axis=1)
@@ -118,10 +172,6 @@
         for owner in range(CBD):
             for b in range(CBD):
                 out[owner, d, b] = total[owner * B:(owner + 1) * B, b * B:(b + 1) * B]
-            store = pltpu.make_async_copy(
-                out.at[owner, d], out_hbm.at[owner, d], out_sem.at[owner, d])
-            store.start()
-            stores.append(store)
 
     def split(j, block, mask):
         high = block * mask
@@ -133,8 +183,11 @@
         split(j, p[j], mask)
     finish(0, 0, FB)
 
-    for q in range(4):
+    for q in (1, 3, 2, 0):
         there = around[q][0]
+        if q == 2:
+            answer(0, around[0][3])
+            answer(2, around[2][3])
 
         @pl.when(there)
         def _():
@@ -150,8 +203,6 @@
 
         finish(q + 1, FB + q * RL, RL)
 
-    for store in stores:
-        store.wait()
     for e in range(4):
         @pl.when(around[e][0])
         def _():
@@ -160,15 +211,18 @@
 
 
 def body(a_blocks, columns, counts, p_blocks, aggregate, readers):
-    smem = pl.BlockSpec(memory_space=pltpu.SMEM)
-    anywhere = pl.BlockSpec(memory_space=pl.ANY)
+    hbm = pl.BlockSpec(memory_space=pltpu.HBM)
     bf16, f32, i32 = jnp.bfloat16, jnp.float32, jnp.int32
     return pl.pallas_call(
         kernel,
-        out_shape=jax.ShapeDtypeStruct((CBD, 5, CBD, B, B), f32),
-        in_specs=[smem] * 4 + [anywhere] * 2,
-        out_specs=anywhere,
+        out_shape=pltpu.VMEM((CBD, 5, CBD, B, B), f32),
+        in_specs=[hbm] * 6,
+        out_specs=pl.BlockSpec(memory_space=pltpu.VMEM),
         scratch_shapes=[
+            pltpu.SMEM((FB, KMAX), i32),
+            pltpu.SMEM((FB,), i32),
+            pltpu.SMEM((FB,), i32),
+            pltpu.SMEM((1, 4, RL), i32),
             pltpu.VMEM((FB, B, B), bf16),
             pltpu.VMEM((FB, KMAX, B, B), bf16),
             pltpu.VMEM((4, RL, B, B), bf16),
@@ -181,18 +235,18 @@
             pltpu.VMEM((SLOTS + 1, B, B), f32),
             pltpu.VMEM((COLS, CBD * B, B), bf16),
             pltpu.VMEM((FB * B, CBD * B), bf16),
-            pltpu.VMEM((CBD, 5, CBD, B, B), f32),
+            pltpu.SemaphoreType.DMA((4,)),
             pltpu.SemaphoreType.DMA,
             pltpu.SemaphoreType.DMA((FB,)),
             pltpu.SemaphoreType.DMA,
-            pltpu.SemaphoreType.DMA((CBD, 5)),
-            pltpu.SemaphoreType.DMA((4,)),
-            pltpu.SemaphoreType.DMA((4,)),
-            pltpu.SemaphoreType.DMA((4,)),
-            pltpu.SemaphoreType.DMA((4,)),
+            pltpu.SemaphoreType.DMA((4,)),
+            pltpu.SemaphoreType.DMA((4,)),
+            pltpu.SemaphoreType.DMA((4,)),
+            pltpu.SemaphoreType.DMA((4,)),
+            pltpu.SemaphoreType.REGULAR((4,)),
         ],
         compiler_params=pltpu.CompilerParams(
-            collective_id=0, has_side_effects=True, vmem_limit_bytes=40 * 1024 * 1024
+            collective_id=0, has_side_effects=True, vmem_limit_bytes=61 * 1024 * 1024
         ),
         cost_estimate=pl.CostEstimate(
             flops=700_000_000, bytes_accessed=3_500_000, transcendentals=0

time: 32.6 us -> 22.6 us (0.69)
  the two profiles are of different devices: /device:TPU:120 before, /device:TPU:108 now
where the time goes in v2:
time: 22.6 us; the launch traced here: 22.4 us
  Pallas kernels  21.4 us (95%)
  local copies, waits for them, and re-layouts  1.06 us (5%)
    pallas_call x1, Pallas kernels, body(): pl.pallas_call(kernel, out_shape=pltpu.VMEM((CBD, 5, CBD, B, B), f32), in...  21.4 us
    unnamed x1, local copies, waits for them, and re-layouts  1.06 us

profile of v2, /device:TPU:108, one launch (start us, length us, event | category | flops | bytes accessed | tf_op | source)
XLA Modules:
  0.0 22.4 jit_solution(14926171524144051199)
XLA Ops:
  0.0 21.4 %coarse_blocks.1 = f32[2,5,2,128,128]{4,3,2,1,0:T(8,128)S(1)} custom-call(s32[8,7]{1,0:T(8,128)} %columns_hbm.1, s32[8]{0:T(128)} %counts_hbm.1, s32[8]{0:T(128)} %aggregate_hbm.1, s32[1,4,6]{2,1,0:T(4,128)} %readers_hbm.1, bf16[8,7,128,128]{3,2,1,0:T(8,128)(2,1)} %a_hbm.1, bf16[8,128,128]{2,1,0:T(8,128)(2,1)} %p_hbm.1), custom_call_target="tpu_custom_call" | custom-call | flops 700000000 | bytes 3500000 | tf_op jit(solution)/shard_map/coarse_blocks/pallas_call | solution.py:216
  21.4 1.1 %copy.8 = f32[2,5,2,128,128]{4,3,2,1,0:T(8,128)} copy(f32[2,5,2,128,128]{4,3,2,1,0:T(8,128)S(1)} %coarse_blocks.1) | data formatting | bytes 2621440

commit v3 on v2

--- a/solution.py
+++ b/solution.py
@@ -37,8 +37,19 @@
     )
 
 
+def spread(row):
+    return jnp.broadcast_to(row, (B, B)).astype(jnp.bfloat16)
+
+
+def split(x, j, block, mask):
+    high = block * mask
+    x[j * B:(j + 1) * B, B:] = high
+    x[j * B:(j + 1) * B, :B] = block - high
+
+
 def kernel(
-    columns_hbm, counts_hbm, aggregate_hbm, readers_hbm, a_hbm, p_hbm, out,
+    columns_hbm, counts_hbm, aggregate_hbm, readers_hbm, a_hbm, p_hbm,
+    out, last, last_blocks, last_mask,
     columns, counts, aggregate, readers, p, a, send, recv, send_mask, recv_mask, keys, links, table, sums, c, x,
     int_sem, p_sem, a_sem, table_sem, send_sem, recv_sem, send_mask_sem, recv_mask_sem, ready,
 ):
@@ -52,24 +63,40 @@
     load_p = pltpu.make_async_copy(p_hbm, p, p_sem)
     load_a = [pltpu.make_async_copy(a_hbm.at[i], a.at[i], a_sem.at[i]) for i in range(FB)]
     load_lists[0].start()
+    load_lists[1].start()
     load_p.start()
-    for copy in load_lists[1:]:
+
+    barrier = pltpu.get_barrier_semaphore()
+    for there, device, later, much in around:
+        @pl.when(there & later)
+        def _():
+            pl.semaphore_signal(barrier, inc=1, device_id=device, device_id_type=MESH)
+    before = [there & jnp.logical_not(later) for there, unused, later, much in around]
+    expected = sum(first.astype(jnp.int32) for first in before)
+
+    @pl.when(expected > 0)
+    def _():
+        pl.semaphore_wait(barrier, expected)
+
+    for e in (1, 0, 2, 3):
+        @pl.when(before[e])
+        def _():
+            pl.semaphore_signal(
+                ready.at[e ^ 1], inc=1, device_id=around[e][1], device_id_type=MESH)
+    for copy in load_lists[2:]:
         copy.start()
-    barrier = pltpu.get_barrier_semaphore()
-    for there, device, later, unused in around:
-        @pl.when(there & later)
-        def _():
-            pl.semaphore_signal(barrier, inc=1, device_id=device, device_id_type=MESH)
 
     sublane = lax.broadcasted_iota(jnp.int32, (8, B), 0)
+    landing = [last_blocks] + [recv.at[n] for n in range(3)]
+    landing_mask = [last_mask] + [recv_mask.at[n] for n in range(3)]
     blocks, masks = [], []
     for e in range(4):
         device = around[e][1]
         blocks.append(pltpu.make_async_remote_copy(
-            src_ref=send.at[e], dst_ref=recv.at[e ^ 1], send_sem=send_sem.at[e],
+            src_ref=send.at[e], dst_ref=landing[e ^ 1], send_sem=send_sem.at[e],
             recv_sem=recv_sem.at[e ^ 1], device_id=device, device_id_type=MESH))
         masks.append(pltpu.make_async_remote_copy(
-            src_ref=send_mask.at[e], dst_ref=recv_mask.at[e ^ 1], send_sem=send_mask_sem.at[e],
+            src_ref=send_mask.at[e], dst_ref=landing_mask[e ^ 1], send_sem=send_mask_sem.at[e],
             recv_sem=recv_mask_sem.at[e ^ 1], device_id=device, device_id_type=MESH))
 
     def pack(e):
@@ -98,26 +125,9 @@
     for copy in load_lists[:2]:
         copy.wait()
     load_p.wait()
-    pack(1)
-    before = [there & jnp.logical_not(later) for there, unused, later, much in around]
-    expected = sum(first.astype(jnp.int32) for first in before)
-
-    @pl.when(expected > 0)
-    def _():
-        pl.semaphore_wait(barrier, expected)
-
-    start(1, before[1])
-    for e in range(4):
-        @pl.when(before[e])
-        def _():
-            pl.semaphore_signal(
-                ready.at[e ^ 1], inc=1, device_id=around[e][1], device_id_type=MESH)
-    pack(0)
-    start(0, before[0])
-    pack(2)
-    start(2, before[2])
-    pack(3)
-    start(3, before[3])
+    for e in (1, 0, 2, 3):
+        pack(e)
+        start(e, before[e])
     for copy in load_a:
         copy.start()
     for copy in load_lists[2:]:
@@ -133,8 +143,8 @@
     row = lax.broadcasted_iota(jnp.int32, (64, B), 0)
     lane = lax.broadcasted_iota(jnp.int32, (64, B), 1)
     by_lane = jnp.sum(jnp.where(row == lane, by_row, 0), axis=0, keepdims=True)
-    before = jnp.where((by_row == by_lane) & (row < lane), row + 1, 0)
-    links[0:1, :] = jnp.max(before, axis=0, keepdims=True)
+    linked = jnp.where((by_row == by_lane) & (row < lane), row + 1, 0)
+    links[0:1, :] = jnp.max(linked, axis=0, keepdims=True)
     links[1:2, :] = jnp.max(jnp.where(by_row == lane, row + 1, 0), axis=0, keepdims=True)
     links[2:, :] = jnp.zeros((6, B), jnp.int32)
     load_table = pltpu.make_async_copy(links, table, table_sem)
@@ -164,7 +174,14 @@
         c[j, B:2 * B, :] = sums[table[1, COLS + j]].astype(jnp.bfloat16)
         return carry
 
-    lax.fori_loop(0, COLS, collect, 0)
+    def collect_last(r, carry):
+        last[r, 0:B, :] = sums[table[1, FB + r]].astype(jnp.bfloat16)
+        last[r, B:2 * B, :] = sums[table[1, COLS + FB + r]].astype(jnp.bfloat16)
+        return carry
+
+    lax.fori_loop(0, FB, collect, 0)
+    lax.fori_loop(FB + RL, COLS, collect, 0)
+    lax.fori_loop(0, RL, collect_last, 0)
 
     def finish(d, first, number):
         left = jnp.concatenate([c[first + j] for j in range(number)], axis=1)
@@ -173,17 +190,12 @@
             for b in range(CBD):
                 out[owner, d, b] = total[owner * B:(owner + 1) * B, b * B:(b + 1) * B]
 
-    def split(j, block, mask):
-        high = block * mask
-        x[j * B:(j + 1) * B, B:] = high
-        x[j * B:(j + 1) * B, :B] = block - high
-
     for j in range(FB):
         mask = jnp.full((B, B), aggregate[j], jnp.int32).astype(jnp.float32).astype(jnp.bfloat16)
-        split(j, p[j], mask)
+        split(x, j, p[j], mask)
     finish(0, 0, FB)
 
-    for q in (1, 3, 2, 0):
+    for q in (1, 3, 2):
         there = around[q][0]
         if q == 2:
             answer(0, around[0][3])
@@ -194,14 +206,25 @@
             blocks[q ^ 1].wait_recv()
             masks[q ^ 1].wait_recv()
             for r in range(RL):
-                mask = jnp.broadcast_to(recv_mask[q, r:r + 1, :], (B, B)).astype(jnp.bfloat16)
-                split(r, recv[q, r], mask)
+                split(x, r, recv[q - 1, r], spread(recv_mask[q - 1, r:r + 1, :]))
 
         @pl.when(jnp.logical_not(there))
         def _():
             x[0:RL * B, :] = jnp.zeros((RL * B, CBD * B), jnp.bfloat16)
 
         finish(q + 1, FB + q * RL, RL)
+
+    there = around[0][0]
+
+    @pl.when(there)
+    def _():
+        blocks[1].wait_recv()
+        masks[1].wait_recv()
+
+    @pl.when(jnp.logical_not(there))
+    def _():
+        last_blocks[...] = jnp.zeros((RL, B, B), jnp.bfloat16)
+        last_mask[...] = jnp.zeros((8, B), jnp.float32)
 
     for e in range(4):
         @pl.when(around[e][0])
@@ -210,14 +233,43 @@
             blocks[e].wait_send()
 
 
+def store_blocks(out, last, last_blocks, last_mask, result, x, piece, out_sem, piece_sem):
+    stores = []
+    for owner in range(CBD):
+        for n, (first, number) in enumerate(((0, 1), (2, 3))):
+            there = pl.ds(first, number)
+            stores.append(pltpu.make_async_copy(
+                out.at[owner, there], result.at[owner, there], out_sem.at[owner, n]))
+    for store in stores:
+        store.start()
+    for r in range(RL):
+        split(x, r, last_blocks[r], spread(last_mask[r:r + 1, :]))
+    left = jnp.concatenate([last[r] for r in range(RL)], axis=1)
+    total = jnp.dot(left, x[...], preferred_element_type=jnp.float32)
+    for owner in range(CBD):
+        for b in range(CBD):
+            piece[owner, b] = total[owner * B:(owner + 1) * B, b * B:(b + 1) * B]
+        stores.append(pltpu.make_async_copy(
+            piece.at[owner], result.at[owner, 1], piece_sem.at[owner]))
+        stores[-1].start()
+    for store in stores:
+        store.wait()
+
+
 def body(a_blocks, columns, counts, p_blocks, aggregate, readers):
     hbm = pl.BlockSpec(memory_space=pltpu.HBM)
+    vmem = pl.BlockSpec(memory_space=pltpu.VMEM)
     bf16, f32, i32 = jnp.bfloat16, jnp.float32, jnp.int32
-    return pl.pallas_call(
+    parts = pl.pallas_call(
         kernel,
-        out_shape=pltpu.VMEM((CBD, 5, CBD, B, B), f32),
+        out_shape=(
+            pltpu.VMEM((CBD, 5, CBD, B, B), f32),
+            pltpu.VMEM((RL, CBD * B, B), bf16),
+            pltpu.VMEM((RL, B, B), bf16),
+            pltpu.VMEM((8, B), f32),
+        ),
         in_specs=[hbm] * 6,
-        out_specs=pl.BlockSpec(memory_space=pltpu.VMEM),
+        out_specs=(vmem,) * 4,
         scratch_shapes=[
             pltpu.SMEM((FB, KMAX), i32),
             pltpu.SMEM((FB,), i32),
@@ -226,9 +278,9 @@
             pltpu.VMEM((FB, B, B), bf16),
             pltpu.VMEM((FB, KMAX, B, B), bf16),
             pltpu.VMEM((4, RL, B, B), bf16),
-            pltpu.VMEM((4, RL, B, B), bf16),
+            pltpu.VMEM((3, RL, B, B), bf16),
             pltpu.VMEM((4, 8, B), f32),
-            pltpu.VMEM((4, 8, B), f32),
+            pltpu.VMEM((3, 8, B), f32),
             pltpu.VMEM((64, B), i32),
             pltpu.VMEM((8, B), i32),
             pltpu.SMEM((8, B), i32),
@@ -246,13 +298,30 @@
             pltpu.SemaphoreType.REGULAR((4,)),
         ],
         compiler_params=pltpu.CompilerParams(
-            collective_id=0, has_side_effects=True, vmem_limit_bytes=61 * 1024 * 1024
+            collective_id=0, has_side_effects=True, vmem_limit_bytes=60 * 1024 * 1024
         ),
         cost_estimate=pl.CostEstimate(
             flops=700_000_000, bytes_accessed=3_500_000, transcendentals=0
         ),
         name="coarse_blocks",
     )(columns, counts, aggregate, readers, a_blocks, p_blocks)
+    return pl.pallas_call(
+        store_blocks,
+        out_shape=jax.ShapeDtypeStruct((CBD, 5, CBD, B, B), f32),
+        in_specs=[vmem] * 4,
+        out_specs=hbm,
+        scratch_shapes=[
+            pltpu.VMEM((RL * B, CBD * B), bf16),
+            pltpu.VMEM((CBD, CBD, B, B), f32),
+            pltpu.SemaphoreType.DMA((CBD, 2)),
+            pltpu.SemaphoreType.DMA((CBD,)),
+        ],
+        compiler_params=pltpu.CompilerParams(vmem_limit_bytes=8 * 1024 * 1024),
+        cost_estimate=pl.CostEstimate(
+            flops=100_000_000, bytes_accessed=1_310_720, transcendentals=0
+        ),
+        name="store_blocks",
+    )(*parts)
 
 
 def solution(mesh):

time: 22.6 us -> 22.3 us (0.987)
  the two profiles are of different devices: /device:TPU:108 before, /device:TPU:120 now
where the time goes in v3:
time: 22.3 us; the launch traced here: 22.1 us
  Pallas kernels  22.1 us (99%)
    pallas_call x1, Pallas kernels, body(): pl.pallas_call(kernel, out_shape=(pltpu.VMEM((CBD, 5, CBD, B, B), f32), p...  21 us
    pallas_call x1, Pallas kernels, body(): pl.pallas_call(store_blocks, out_shape=jax.ShapeDtypeStruct((CBD, 5, CBD,...  1.14 us

profile of v3, /device:TPU:120, one launch (start us, length us, event | category | flops | bytes accessed | tf_op | source)
XLA Modules:
  0.0 22.1 jit_solution(3502172862552539289)
XLA Ops:
  0.0 21.0 %coarse_blocks.1 = (f32[2,5,2,128,128]{4,3,2,1,0:T(8,128)S(1)}, bf16[6,256,128]{2,1,0:T(8,128)(2,1)S(1)}, bf16[6,128,128]{2,1,0:T(8,128)(2,1)S(1)}, f32[8,128]{1,0:T(8,128)S(1)}) custom-call(s32[8,7]{1,0:T(8,128)} %columns_hbm.1, s32[8]{0:T(128)} %counts_hbm.1, s32[8]{0:T(128)} %aggregate_hbm.1, s32[1,4,6]{2,1,0:T(4,128)} %readers_hbm.1, ...), custom_call_target="tpu_custom_call" | custom-call | flops 700000000 | bytes 3500000 | tf_op jit(solution)/shard_map/coarse_blocks/pallas_call | solution.py:263
  21.0 1.1 %store_blocks.1 = f32[2,5,2,128,128]{4,3,2,1,0:T(8,128)} custom-call(f32[2,5,2,128,128]{4,3,2,1,0:T(8,128)S(1)} %get-tuple-element.9.out, bf16[6,256,128]{2,1,0:T(8,128)(2,1)S(1)} %get-tuple-element.10.last, bf16[6,128,128]{2,1,0:T(8,128)(2,1)S(1)} %get-tuple-element.11.last_blocks, f32[8,128]{1,0:T(8,128)S(1)} %get-tuple-element.12.last_mask), custom_call_target="tpu_custom_call" | custom-call | flops 100000000 | bytes 1310720 | tf_op jit(solution)/shard_map/store_blocks/pallas_call | solution.py:308

commit v4 on v3

--- a/solution.py
+++ b/solution.py
@@ -62,9 +62,9 @@
     ]
     load_p = pltpu.make_async_copy(p_hbm, p, p_sem)
     load_a = [pltpu.make_async_copy(a_hbm.at[i], a.at[i], a_sem.at[i]) for i in range(FB)]
+    load_p.start()
     load_lists[0].start()
     load_lists[1].start()
-    load_p.start()
 
     barrier = pltpu.get_barrier_semaphore()
     for there, device, later, much in around:
@@ -100,17 +100,23 @@
             recv_sem=recv_mask_sem.at[e ^ 1], device_id=device, device_id_type=MESH))
 
     def pack(e):
+        for r, block in enumerate(listed[e]):
+            send[e, r] = p[block]
+
+    def pack_mask(e):
         mask = jnp.zeros((8, B), jnp.int32)
         for r in range(RL):
-            block = readers[0, e, r]
-            send[e, r] = p[block]
-            mask = jnp.where(sublane == r, aggregate[block], mask)
+            mask = jnp.where(sublane == r, aggregate[readers[0, e, r]], mask)
         send_mask[e] = mask.astype(jnp.float32)
+
+    def start_mask(e, condition):
+        @pl.when(around[e][0] & condition)
+        def _():
+            masks[e].start()
 
     def start(e, condition):
         @pl.when(around[e][0] & condition)
         def _():
-            masks[e].start()
             blocks[e].start()
 
     def answer(e, condition):
@@ -124,6 +130,10 @@
 
     for copy in load_lists[:2]:
         copy.wait()
+    for e in (1, 0, 2, 3):
+        pack_mask(e)
+        start_mask(e, before[e])
+    listed = [[readers[0, e, r] for r in range(RL)] for e in range(4)]
     load_p.wait()
     for e in (1, 0, 2, 3):
         pack(e)
@@ -214,6 +224,12 @@
 
         finish(q + 1, FB + q * RL, RL)
 
+    for e in range(4):
+        @pl.when(around[e][0])
+        def _():
+            masks[e].wait_send()
+            blocks[e].wait_send()
+
     there = around[0][0]
 
     @pl.when(there)
@@ -225,12 +241,6 @@
     def _():
         last_blocks[...] = jnp.zeros((RL, B, B), jnp.bfloat16)
         last_mask[...] = jnp.zeros((8, B), jnp.float32)
-
-    for e in range(4):
-        @pl.when(around[e][0])
-        def _():
-            masks[e].wait_send()
-            blocks[e].wait_send()
 
 
 def store_blocks(out, last, last_blocks, last_mask, result, x, piece, out_sem, piece_sem):

time: 22.3 us -> 22.2 us (level)
  the two profiles are of different devices: /device:TPU:120 before, /device:TPU:126 now
where the time goes in v4:
time: 22.2 us; the launch traced here: 22 us
  Pallas kernels  22 us (99%)
    pallas_call x1, Pallas kernels, body(): pl.pallas_call(kernel, out_shape=(pltpu.VMEM((CBD, 5, CBD, B, B), f32), p...  20.9 us
    pallas_call x1, Pallas kernels, body(): pl.pallas_call(store_blocks, out_shape=jax.ShapeDtypeStruct((CBD, 5, CBD,...  1.14 us

profile of v4, /device:TPU:126, one launch (start us, length us, event | category | flops | bytes accessed | tf_op | source)
XLA Modules:
  0.0 22.0 jit_solution(17735811906406532539)
XLA Ops:
  0.0 20.9 %coarse_blocks.1 = (f32[2,5,2,128,128]{4,3,2,1,0:T(8,128)S(1)}, bf16[6,256,128]{2,1,0:T(8,128)(2,1)S(1)}, bf16[6,128,128]{2,1,0:T(8,128)(2,1)S(1)}, f32[8,128]{1,0:T(8,128)S(1)}) custom-call(s32[8,7]{1,0:T(8,128)} %columns_hbm.1, s32[8]{0:T(128)} %counts_hbm.1, s32[8]{0:T(128)} %aggregate_hbm.1, s32[1,4,6]{2,1,0:T(4,128)} %readers_hbm.1, ...), custom_call_target="tpu_custom_call" | custom-call | flops 700000000 | bytes 3500000 | tf_op jit(solution)/shard_map/coarse_blocks/pallas_call | solution.py:273
  20.9 1.1 %store_blocks.1 = f32[2,5,2,128,128]{4,3,2,1,0:T(8,128)} custom-call(f32[2,5,2,128,128]{4,3,2,1,0:T(8,128)S(1)} %get-tuple-element.9.out, bf16[6,256,128]{2,1,0:T(8,128)(2,1)S(1)} %get-tuple-element.10.last, bf16[6,128,128]{2,1,0:T(8,128)(2,1)S(1)} %get-tuple-element.11.last_blocks, f32[8,128]{1,0:T(8,128)S(1)} %get-tuple-element.12.last_mask), custom_call_target="tpu_custom_call" | custom-call | flops 100000000 | bytes 1310720 | tf_op jit(solution)/shard_map/store_blocks/pallas_call | solution.py:318

commit v5 on v4

--- a/solution.py
+++ b/solution.py
@@ -16,6 +16,7 @@
 COLS = FB + 4 * RL
 SLOTS = FB * KMAX
 LINE = 8
+PART = 3
 
 
 def neighbours():
@@ -135,7 +136,18 @@
         start_mask(e, before[e])
     listed = [[readers[0, e, r] for r in range(RL)] for e in range(4)]
     load_p.wait()
-    for e in (1, 0, 2, 3):
+    for r in range(0, RL, PART):
+        for block in range(r, r + PART):
+            send[1, block] = p[listed[1][block]]
+
+        @pl.when(before[1])
+        def _():
+            pltpu.make_async_remote_copy(
+                src_ref=send.at[1, pl.ds(r, PART)], dst_ref=last_blocks.at[pl.ds(r, PART)],
+                send_sem=send_sem.at[1], recv_sem=recv_sem.at[0],
+                device_id=around[1][1], device_id_type=MESH).start()
+
+    for e in (0, 2, 3):
         pack(e)
         start(e, before[e])
     for copy in load_a:

time: 22.2 us -> 22.2 us (level)
  no operation moved by 1% of the time
where the time goes in v5:
time: 22.2 us; the launch traced here: 22 us
  Pallas kernels  22 us (99%)
    pallas_call x1, Pallas kernels, body(): pl.pallas_call(kernel, out_shape=(pltpu.VMEM((CBD, 5, CBD, B, B), f32), p...  20.9 us
    pallas_call x1, Pallas kernels, body(): pl.pallas_call(store_blocks, out_shape=jax.ShapeDtypeStruct((CBD, 5, CBD,...  1.14 us

profile of v5, /device:TPU:126, one launch (start us, length us, event | category | flops | bytes accessed | tf_op | source)
XLA Modules:
  0.0 22.0 jit_solution(5566584990174265523)
XLA Ops:
  0.0 20.9 %coarse_blocks.1 = (f32[2,5,2,128,128]{4,3,2,1,0:T(8,128)S(1)}, bf16[6,256,128]{2,1,0:T(8,128)(2,1)S(1)}, bf16[6,128,128]{2,1,0:T(8,128)(2,1)S(1)}, f32[8,128]{1,0:T(8,128)S(1)}) custom-call(s32[8,7]{1,0:T(8,128)} %columns_hbm.1, s32[8]{0:T(128)} %counts_hbm.1, s32[8]{0:T(128)} %aggregate_hbm.1, s32[1,4,6]{2,1,0:T(4,128)} %readers_hbm.1, ...), custom_call_target="tpu_custom_call" | custom-call | flops 700000000 | bytes 3500000 | tf_op jit(solution)/shard_map/coarse_blocks/pallas_call | solution.py:285
  20.9 1.1 %store_blocks.1 = f32[2,5,2,128,128]{4,3,2,1,0:T(8,128)} custom-call(f32[2,5,2,128,128]{4,3,2,1,0:T(8,128)S(1)} %get-tuple-element.9.out, bf16[6,256,128]{2,1,0:T(8,128)(2,1)S(1)} %get-tuple-element.10.last, bf16[6,128,128]{2,1,0:T(8,128)(2,1)S(1)} %get-tuple-element.11.last_blocks, f32[8,128]{1,0:T(8,128)S(1)} %get-tuple-element.12.last_mask), custom_call_target="tpu_custom_call" | custom-call | flops 100000000 | bytes 1310720 | tf_op jit(solution)/shard_map/store_blocks/pallas_call | solution.py:330
